TPU v7x, 32 devices: a whole 2x2x4 slice. The times are simulated.
32 devices in a mesh: basin: 8 (over z, x), event: 4 (over y, core).
Axes of the slice: x: 2, y: 2, z: 4, core: 2. Of those that a mesh axis runs over, the one named last changes fastest.
Arguments:
- reach_attrs: bfloat16 [12288, 32], P('basin'), may hold values from -6 to 6
- w_first: bfloat16 [32, 768], replicated, may hold values from -1 to 1
- b_first: float32 [768], replicated, may hold values from -3 to 3
- w_second: bfloat16 [768, 768], replicated, may hold values from -0.21875 to 0.21875
- b_second: float32 [768], replicated, may hold values from -3 to 3
- w_out: bfloat16 [768], replicated, may hold values from -0.21875 to 0.21875
- section_factor: float32 [10], replicated, may hold values from 0.5 to 2
- bed_slope: float32 [12288], P('basin'), may hold values from 0.0001 to 0.004
- seg_count: int32 [12288], P('basin'), may hold values from 1 to 8
- section_class: int32 [12288], P('basin'), may hold values from 0 to 9
- down_local: int32 [12288], P('basin'), may hold values from 0 to 1536, as said below
- send_list: int32 [8, 8, 24], P('basin'), may hold values from 0 to 1536, as said below
- recv_list: int32 [8, 8, 24], P('basin'), may hold values from 0 to 1536, as said below
- area_start: float32 [128, 12288], P('event', 'basin'), may hold values from 0.2 to 2
- lateral: float32 [3, 128, 12288], P(None, 'event', 'basin'), may hold values from 0.05 to 1
- cotangent: float32 [128, 12288], P('event', 'basin'), may hold values from -6 to 6
Outputs:
- outflow: float32 [128, 12288], P('event', 'basin')
- grad_lateral: float32 [3, 128, 12288], P(None, 'event', 'basin')
- grad_w_first: float32 [32, 768], replicated
- grad_b_first: float32 [768], replicated
- grad_w_second: float32 [768, 768], replicated
- grad_b_second: float32 [768], replicated
- grad_w_out: float32 [768], replicated
Inputs may be any that keep to these rules, and one draw needn't show every extreme that they name: `down_local`: the downstream reach of a reach in its own sub-basin, as a local index 1 to 8 above the reach's own; 1536 where the reach drains into another sub-basin (it is then listed in send_list) or leaves the network. send_list[s, d, c] is a local reach of sub-basin s whose end flow enters sub-basin d, or 1536 for an empty slot; live slots come first in each list and no reach is listed twice. Only the lists from s to (s + 1), (s + 2), (s + 4) and (s + 7) mod 8 can hold live slots; those to (s + 1), (s + 4) and (s + 7) are always full, the one to (s + 2) is empty or holds 12 or more. One sub-basin receives 24 from each of the four sub-basins that can drain into it. recv_list[d, s, c] is the local reach of sub-basin d that receives slot c of send_list[s, d], and is 1536 exactly where that slot is empty; no reach is a target twice.
All inputs are finite; a program needn't handle non-finite values.
Results may differ from a plain program's by a relative error of at most 0.02.
Values sent between devices are 32-bit elements; how exact they have to be, the bound alone decides.
A program may use at most 64 MiB of HBM per device.

v0:
```python
import math

import jax
import jax.numpy as jnp
from jax import lax
from jax.sharding import PartitionSpec as P

STEPS = 3


def emit(area_now, flow_rate):
    return flow_rate * area_now ** (5.0 / 3.0)


def advance(area_now, inflow, lateral_now, flow_rate, beta_step):
    return (area_now + beta_step * (inflow + lateral_now)) / (
        1.0 + beta_step * flow_rate * area_now ** (2.0 / 3.0)
    )


def network_forward(reach_attrs, w_first, b_first, w_second, b_second, w_out):
    tanh_one = jnp.tanh(jnp.dot(reach_attrs, w_first, preferred_element_type=jnp.float32) + b_first)
    hid_one = tanh_one.astype(jnp.bfloat16)
    tanh_two = jnp.tanh(jnp.dot(hid_one, w_second, preferred_element_type=jnp.float32) + b_second)
    hid_two = tanh_two.astype(jnp.bfloat16)
    squash = jax.nn.sigmoid(jnp.dot(hid_two, w_out, preferred_element_type=jnp.float32))
    return (0.02 + 0.08 * squash, (tanh_one, hid_one, tanh_two, hid_two, squash))


def upper_grads(saved_acts, w_out, g_rough, scale):
    tanh_one, hid_one, tanh_two, hid_two, squash = saved_acts
    g_logit = (g_rough * scale * 0.08 * squash * (1.0 - squash)).astype(jnp.bfloat16)
    grad_w_out = jnp.dot(g_logit, hid_two, preferred_element_type=jnp.float32)
    g_pre_two = (
        g_logit.astype(jnp.float32)[:, None]
        * w_out.astype(jnp.float32)[None, :]
        * (1.0 - tanh_two * tanh_two)
    )
    g_two = g_pre_two.astype(jnp.bfloat16)
    grad_w_second = jnp.dot(hid_one.T, g_two, preferred_element_type=jnp.float32)
    return (g_two, (grad_w_out, jnp.sum(g_pre_two, axis=0), grad_w_second))


def lower_grads(reach_attrs, w_second, saved_acts, g_two):
    tanh_one = saved_acts[0]
    g_pre_one = jnp.dot(g_two, w_second.T, preferred_element_type=jnp.float32) * (
        1.0 - tanh_one * tanh_one
    )
    grad_w_first = jnp.dot(
        reach_attrs.T, g_pre_one.astype(jnp.bfloat16), preferred_element_type=jnp.float32
    )
    return (jnp.sum(g_pre_one, axis=0), grad_w_first)


def body(
    reach_attrs,
    w_first,
    b_first,
    w_second,
    b_second,
    w_out,
    section_factor,
    bed_slope,
    seg_count,
    section_class,
    down_local,
    send_list,
    recv_list,
    area_start,
    lateral,
    cotangent,
):
    local_events, local_reaches = area_start.shape
    class_total = section_factor.shape[0]
    one_hot = (section_class[:, None] == jnp.arange(class_total, dtype=jnp.int32)[None, :]).astype(
        jnp.float32
    )
    k_base = jnp.sqrt(bed_slope) * jnp.sum(one_hot * section_factor[None, :], axis=1)
    beta_step = 1.0 / seg_count.astype(jnp.float32)
    senders = send_list.reshape(-1)
    targets = recv_list.reshape(-1)
    zero_column = jnp.zeros((local_events, 1), jnp.float32)
    roughness, saved_acts = network_forward(
        reach_attrs, w_first, b_first, w_second, b_second, w_out
    )

    def rate_of(rough_all):
        return k_base / rough_all

    flow_rate, pull_rate = jax.vjp(rate_of, roughness)

    def step_of(area_now, inflow, lateral_now, rate_now):
        return advance(area_now, inflow, lateral_now, rate_now, beta_step)

    areas = [area_start]
    inflows = []
    flow_now = emit(area_start, flow_rate)
    for step in range(STEPS):
        confluence_padded = jnp.concatenate([flow_now, zero_column], axis=1)
        confluence_inflow = (
            jnp.zeros((local_events, local_reaches + 1), jnp.float32)
            .at[:, down_local]
            .add(flow_now)
        )
        arrived = lax.all_to_all(
            confluence_padded[:, senders], "basin", split_axis=1, concat_axis=1, tiled=True
        )
        confluence_inflow = confluence_inflow.at[:, targets].add(arrived)
        inflow = confluence_inflow[:, :local_reaches]
        inflows.append(inflow)
        area_next = step_of(areas[step], inflow, lateral[step], flow_rate)
        areas.append(area_next)
        flow_now = emit(area_next, flow_rate)
    g_area, g_rate = jax.vjp(emit, areas[STEPS], flow_rate)[1](cotangent)
    grads_lat = [None] * STEPS
    for step in reversed(range(STEPS)):
        g_prev, g_inflow, g_lateral, g_rate_step = jax.vjp(
            step_of, areas[step], inflows[step], lateral[step], flow_rate
        )[1](g_area)
        grads_lat[step] = g_lateral
        padded = jnp.concatenate([g_inflow, zero_column], axis=1)
        g_flow = jnp.zeros((local_events, local_reaches + 1), jnp.float32)
        returned = lax.all_to_all(
            padded[:, targets], "basin", split_axis=1, concat_axis=1, tiled=True
        )
        g_flow = g_flow.at[:, senders].add(returned)
        g_flow = g_flow[:, :local_reaches] + padded[:, down_local]
        g_emit_area, g_emit_rate = jax.vjp(emit, areas[step], flow_rate)[1](g_flow)
        g_area = g_prev + g_emit_area
        g_rate = g_rate + g_rate_step + g_emit_rate
    grad_lateral = jnp.stack(grads_lat, axis=0)
    g_rough = pull_rate(g_rate)[0]
    scale = 32.0 / math.sqrt(
        local_events * lax.axis_size("event") * local_reaches * lax.axis_size("basin")
    )
    g_two, upper = upper_grads(saved_acts, w_out, g_rough, scale)
    upper = lax.psum((upper[0], upper[1], upper[2]), ("basin", "event"))
    lower = lax.psum(lower_grads(reach_attrs, w_second, saved_acts, g_two), ("basin", "event"))
    grad_w_out, grad_b_second, grad_w_second = upper
    grad_b_first, grad_w_first = lower
    return (
        flow_now,
        grad_lateral,
        grad_w_first,
        grad_b_first,
        grad_w_second,
        grad_b_second,
        grad_w_out,
    )


def solution(mesh):
    return jax.shard_map(
        body,
        mesh=mesh,
        in_specs=(
            P("basin", None),
            P(),
            P(),
            P(),
            P(),
            P(),
            P(),
            P("basin"),
            P("basin"),
            P("basin"),
            P("basin"),
            P("basin", None, None),
            P("basin", None, None),
            P("event", "basin"),
            P(None, "event", "basin"),
            P("event", "basin"),
        ),
        out_specs=(P("event", "basin"), P(None, "event", "basin"), P(), P(), P(), P(), P()),
        check_vma=False,
    )
```

profile of v0, /device:TPU:21, one launch (start us, length us, event | category | flops | bytes accessed | tf_op | source)
XLA Modules:
  0.0 330.5 jit_solution(14651421957676418809)
XLA Ops:
  8.0 1.7 fusion.52
  9.9 2.1 fusion.13
  11.9 2.1 copy-done.1
  18.8 5.6 %all-to-all-start = ((f32[8,1,768]{2,1,0:T(1,128)}), f32[8,1,768]{2,1,0:T(1,128)}, u32[]{:S(2)}, u32[]{:S(2)}) async-start(f32[8,1,768]{2,1,0:T(1,128)} %reshape.288), calls=%async_computation | async-start | bytes 49152 | tf_op jit(solution)/shard_map/all_to_all | solution.py:105
  24.5 1.3 compare_select_fusion
  27.4 9.0 %scatter_custom_fusion = f32[32,1537]{0,1:T(8,128)S(1)} fusion(s32[1536]{0:T(1024)} %compare_select_fusion, f32[1536,32]{1,0:T(8,128)S(1)} %copy.57, f32[]{:T(128)} %constant.11.clone.1), kind=kCustom, calls=%fused_computation.44 | custom fusion | flops 49152 | bytes 197248 | tf_op jit(solution)/shard_map/scatter-add | solution.py:103
  36.9 1.4 reduce.4
  38.5 2.1 scatter_fusion
  40.9 1.8 power_multiply_fusion.2
  43.0 0.9 concatenate.19.clone
  43.9 2.0 gather_fusion.1
  46.6 5.4 %all-to-all-start.1 = ((f32[8,1,768]{2,1,0:T(1,128)}), f32[8,1,768]{2,1,0:T(1,128)S(1)}, u32[]{:S(2)}, u32[]{:S(2)}) async-start(f32[8,1,768]{2,1,0:T(1,128)} %reshape.290), calls=%async_computation.1 | async-start | bytes 49152 | tf_op jit(solution)/shard_map/all_to_all | solution.py:105
  52.0 1.2 copy.60
  53.2 9.3 %scatter_custom_fusion.2 = f32[32,1537]{0,1:T(8,128)S(1)} fusion(s32[1536]{0:T(1024)} %compare_select_fusion, f32[1536,32]{1,0:T(8,128)} %copy.60, f32[]{:T(128)} %constant.11.clone.1), kind=kCustom, calls=%fused_computation.42 | custom fusion | flops 49152 | bytes 197248 | tf_op jit(solution)/shard_map/scatter-add | solution.py:103
  63.3 2.1 scatter_fusion.1
  65.7 1.4 power_multiply_fusion.1
  67.4 0.9 concatenate.20.clone
  68.4 2.0 gather_fusion.2
  71.0 5.4 %all-to-all-start.2 = ((f32[8,1,768]{2,1,0:T(1,128)}), f32[8,1,768]{2,1,0:T(1,128)S(1)}, u32[]{:S(2)}, u32[]{:S(2)}) async-start(f32[8,1,768]{2,1,0:T(1,128)} %reshape.292), calls=%async_computation.2 | async-start | bytes 49152 | tf_op jit(solution)/shard_map/all_to_all | solution.py:105
  76.5 1.3 pad_clamp_fusion.1
  77.7 1.2 copy.63
  78.9 9.3 %scatter_custom_fusion.4 = f32[32,1537]{0,1:T(8,128)S(1)} fusion(s32[1536]{0:T(1024)} %compare_select_fusion, f32[1536,32]{1,0:T(8,128)} %copy.63, f32[]{:T(128)} %constant.11.clone.1), kind=kCustom, calls=%fused_computation.40 | custom fusion | flops 49152 | bytes 197248 | tf_op jit(solution)/shard_map/scatter-add | solution.py:103
  89.0 2.1 scatter_fusion.2
  91.1 0.9 slice.59
  92.0 1.4 copy.80
  93.4 1.0 fusion.40
  95.1 1.2 copy.87
  96.3 1.2 concatenate.21.clone
  97.5 1.4 gather_fusion.3
  98.9 1.6 reshape.294
  100.5 5.4 %all-to-all-start.3 = ((f32[8,1,768]{2,1,0:T(1,128)}), f32[8,1,768]{2,1,0:T(1,128)}, u32[]{:S(2)}, u32[]{:S(2)}) async-start(f32[8,1,768]{2,1,0:T(1,128)} %reshape.294), calls=%async_computation.3 | async-start | bytes 49152 | tf_op jit(solution)/shard_map/all_to_all | solution.py:123
  105.9 1.3 pad_clamp_fusion
  107.2 4.0 %gather_fusion.4 = f32[1536,32]{1,0:T(8,128)} fusion(f32[32,1537]{0,1:T(8,128)S(1)} %concatenate.21.clone, s32[2048]{0:T(1024)} %pad_clamp_fusion), kind=kCustom, calls=%fused_computation.4 | custom fusion | bytes 399360 | tf_op jit(solution)/shard_map/gather | solution.py:127
  111.2 2.0 copy.69
  113.3 1.4 reduce.7
  115.4 2.1 scatter_custom_fusion.6
  117.5 0.9 slice.60
  118.5 1.4 copy.81
  119.8 3.3 fusion.41
  123.8 1.2 copy.88
  124.9 1.2 concatenate.22.clone
  126.1 1.4 gather_fusion.5
  127.6 1.6 reshape.296
  129.1 5.4 %all-to-all-start.4 = ((f32[8,1,768]{2,1,0:T(1,128)}), f32[8,1,768]{2,1,0:T(1,128)}, u32[]{:S(2)}, u32[]{:S(2)}) async-start(f32[8,1,768]{2,1,0:T(1,128)} %reshape.296), calls=%async_computation.4 | async-start | bytes 49152 | tf_op jit(solution)/shard_map/all_to_all | solution.py:123
  134.6 4.0 %gather_fusion.6 = f32[1536,32]{1,0:T(8,128)} fusion(f32[32,1537]{0,1:T(8,128)S(1)} %concatenate.22.clone, s32[2048]{0:T(1024)} %pad_clamp_fusion), kind=kCustom, calls=%fused_computation.6 | custom fusion | bytes 399360 | tf_op jit(solution)/shard_map/gather | solution.py:127
  138.6 2.1 copy.73
  140.6 1.4 reduce.8
  142.8 2.3 scatter_custom_fusion.7
  145.1 0.9 slice.61
  146.0 1.4 copy.82
  147.4 3.2 multiply_reduce_fusion.4
  150.6 1.0 divide_multiply_fusion
  153.6 5.4 %all-to-all-start.5 = ((f32[8,1,768]{2,1,0:T(1,128)}), f32[8,1,768]{2,1,0:T(1,128)S(1)}, u32[]{:S(2)}, u32[]{:S(2)}) async-start(f32[8,1,768]{2,1,0:T(1,128)} %reshape.298), calls=%async_computation.5 | async-start | bytes 49152 | tf_op jit(solution)/shard_map/all_to_all | solution.py:123
  159.7 3.0 gather_fusion.8
  163.7 1.9 scatter_custom_fusion.8
  166.2 7.0 %fusion.51 = (f32[768]{0:T(1024)S(1)}, bf16[1536,768]{1,0:T(8,128)(2,1)S(1)}) fusion(f32[1536,768]{1,0:T(8,128)} %copy-done.3, f32[768]{0:T(1024)S(1)} %copy-done.37, bf16[768,768]{1,0:T(8,128)(2,1)S(1)} %copy-done, f32[1536,768]{1,0:T(8,128)} %copy-done.1, f32[768]{0:T(1024)S(1)} %convert_element_type.30, f32[1536]{0:T(1024)S(1)} %get-tuple-element.38, ...), kind=kOutput, calls=%fused_computation.102 | convolution fusion | flops 1826094336 | bytes 12994560 | tf_op jit(solution)/shard_map/dot_general | solution.py:46
  173.2 6.2 %fusion.11 = f32[768,768]{1,0:T(8,128)} fusion(f32[1536,768]{1,0:T(8,128)} %copy-done.3, f32[768]{0:T(1024)S(1)} %copy-done.37, f32[1536,768]{1,0:T(8,128)S(1)} %bitcast.127, f32[768]{0:T(1024)S(1)} %convert_element_type.30, f32[1536]{0:T(1024)S(1)} %get-tuple-element.38, f32[768]{0:T(1024)S(1)} %copy-done.20), kind=kOutput, calls=%fused_computation.31 | convolution fusion | flops 1821376512 | bytes 11811840 | tf_op jit(solution)/shard_map/dot_general | solution.py:40
  179.4 1.2 fusion.6
  181.5 3.1 convolution_reduce_fusion.1
  184.6 3.4 %fusion.2 = f32[768]{0:T(1024)S(1)} fusion(f32[1536,768]{1,0:T(8,128)} %copy-done.1, f32[768]{0:T(1024)S(1)} %convert_element_type.30, f32[1536]{0:T(1024)S(1)} %get-tuple-element.38, f32[768]{0:T(1024)S(1)} %copy-done.20), kind=kLoop, calls=%fused_computation.24 | loop fusion | flops 7077120 | bytes 4733952 | tf_op jit(solution)/shard_map/reduce_sum | solution.py:41
  188.0 44.0 %all-reduce.6 = (f32[768]{0:T(1024)}, f32[768]{0:T(1024)}, f32[768]{0:T(1024)}) all-reduce(f32[768]{0:T(1024)S(1)} %get-tuple-element.54, f32[768]{0:T(1024)S(1)} %fusion.2, f32[768]{0:T(1024)S(1)} %convolution_reduce_fusion.1), channel_id=1, replica_groups=mesh['basin'=8,'event'=4] {'basin','event'}, use_global_device_ids=true, to_apply=%region_19.0 | all-reduce | flops 2304 | bytes 18432 | tf_op jit(solution)/shard_map/psum | solution.py:138
  232.0 86.9 %all-reduce.10.cloned.1.call-done = (f32[32,768]{1,0:T(8,128)}, f32[768,768]{1,0:T(8,128)}) async-done(((f32[32,768]{1,0:T(8,128)}, f32[768,768]{1,0:T(8,128)}), (f32[32,768]{1,0:T(8,128)}, f32[768,768]{1,0:T(8,128)})) %all-reduce.10.cloned.1.call-update) | async-done | bytes 2457616 | tf_op jit(solution)/shard_map/psum | solution.py:138
  318.9 1.5 copy.95
  320.5 3.2 copy.96
  (134 shorter events, 19.8 us)
Async XLA Ops:
  7.2 2.7 copy-start
  7.2 2.5 copy-start.35
  7.2 2.5 copy-start.32
  7.2 2.6 copy-start.36
  9.7 2.2 copy-start.3
  9.8 5.0 %copy-start.18 = (f32[1536]{0:T(1024)}, f32[1536]{0:T(1024)S(1)}, u32[]{:S(2)}) copy-start(f32[1536]{0:T(1024)S(1)} %select_reduce_fusion) | copy-start | bytes 18436
  9.9 4.2 %copy-start.20 = (f32[768]{0:T(1024)S(1)}, f32[768]{0:T(1024)}, u32[]{:S(2)}) copy-start(f32[768]{0:T(1024)} %param.20) | copy-start | bytes 9220
  11.9 2.1 copy-start.1
  14.1 0.8 copy-start.27
  14.1 0.8 copy-start.29
  14.1 1.5 copy-start.2
  14.1 1.8 copy-start.33
  14.9 0.6 copy-start.16
  14.9 26.0 %copy-start.4 = (f32[3,32,1536]{2,1,0:T(8,128)S(1)}, f32[3,32,1536]{2,1,0:T(8,128)}, u32[]{:S(2)}) copy-start(f32[3,32,1536]{2,1,0:T(8,128)} %param.30) | copy-start | bytes 1769476
  16.0 0.6 copy-start.34
  18.8 17.6 %all-to-all-start = ((f32[8,1,768]{2,1,0:T(1,128)}), f32[8,1,768]{2,1,0:T(1,128)}, u32[]{:S(2)}, u32[]{:S(2)}) async-start(f32[8,1,768]{2,1,0:T(1,128)} %reshape.288), calls=%async_computation | async-start | bytes 49152 | tf_op jit(solution)/shard_map/all_to_all | solution.py:105
  40.9 1.8 copy-start.11
  40.9 22.4 %copy-start.31 = (s32[192,1]{0,1:T(1,128)S(1)}, s32[192,1]{0,1:T(1,128)}, u32[]{:S(2)}) copy-start(s32[192,1]{0,1:T(1,128)} %compare_select_fusion.2) | copy-start | bytes 2308
  46.6 15.9 %all-to-all-start.1 = ((f32[8,1,768]{2,1,0:T(1,128)}), f32[8,1,768]{2,1,0:T(1,128)S(1)}, u32[]{:S(2)}, u32[]{:S(2)}) async-start(f32[8,1,768]{2,1,0:T(1,128)} %reshape.290), calls=%async_computation.1 | async-start | bytes 49152 | tf_op jit(solution)/shard_map/all_to_all | solution.py:105
  65.7 1.4 copy-start.12
  65.7 27.7 %copy-start.6 = (f32[32,1536]{1,0:T(8,128)S(1)}, f32[32,1536]{1,0:T(8,128)}, u32[]{:S(2)}) copy-start(f32[32,1536]{1,0:T(8,128)} %param.31) | copy-start | bytes 589828
  65.7 27.7 %copy-start.13 = (f32[1536]{0:T(1024)S(1)}, f32[1536]{0:T(1024)}, u32[]{:S(2)}) copy-start(f32[1536]{0:T(1024)} %get-tuple-element.49) | copy-start | bytes 18436
  65.7 27.7 %copy-start.14 = (f32[1536]{0:T(1024)S(1)}, f32[1536]{0:T(1024)}, u32[]{:S(2)}) copy-start(f32[1536]{0:T(1024)} %get-tuple-element.53) | copy-start | bytes 18436
  71.0 17.2 %all-to-all-start.2 = ((f32[8,1,768]{2,1,0:T(1,128)}), f32[8,1,768]{2,1,0:T(1,128)S(1)}, u32[]{:S(2)}, u32[]{:S(2)}) async-start(f32[8,1,768]{2,1,0:T(1,128)} %reshape.292), calls=%async_computation.2 | async-start | bytes 49152 | tf_op jit(solution)/shard_map/all_to_all | solution.py:105
  94.4 0.7 copy-start.7
  94.4 25.4 %copy-start.5 = (f32[32,1536]{1,0:T(8,128)S(1)}, f32[32,1536]{1,0:T(8,128)}, u32[]{:S(2)}) copy-start(f32[32,1536]{1,0:T(8,128)} %get-tuple-element.48) | copy-start | bytes 589828
  100.5 12.8 %all-to-all-start.3 = ((f32[8,1,768]{2,1,0:T(1,128)}), f32[8,1,768]{2,1,0:T(1,128)}, u32[]{:S(2)}, u32[]{:S(2)}) async-start(f32[8,1,768]{2,1,0:T(1,128)} %reshape.294), calls=%async_computation.3 | async-start | bytes 49152 | tf_op jit(solution)/shard_map/all_to_all | solution.py:123
  123.1 0.7 copy-start.9
  129.1 11.5 %all-to-all-start.4 = ((f32[8,1,768]{2,1,0:T(1,128)}), f32[8,1,768]{2,1,0:T(1,128)}, u32[]{:S(2)}, u32[]{:S(2)}) async-start(f32[8,1,768]{2,1,0:T(1,128)} %reshape.296), calls=%async_computation.4 | async-start | bytes 49152 | tf_op jit(solution)/shard_map/all_to_all | solution.py:123
  151.9 14.2 %copy-start.17 = (f32[1536]{0:T(1024)S(1)}, f32[1536]{0:T(1024)}, u32[]{:S(2)}) copy-start(f32[1536]{0:T(1024)} %copy-done.16) | copy-start | bytes 18436
  151.9 14.2 %copy-start.19 = (f32[1536]{0:T(1024)S(1)}, f32[1536]{0:T(1024)}, u32[]{:S(2)}) copy-start(f32[1536]{0:T(1024)} %copy-done.18) | copy-start | bytes 18436
  151.9 14.2 %copy-start.21 = (f32[1536]{0:T(1024)S(1)}, f32[1536]{0:T(1024)}, u32[]{:S(2)}) copy-start(f32[1536]{0:T(1024)} %get-tuple-element.51) | copy-start | bytes 18436
  151.9 14.2 %copy-start.22 = (f32[1536]{0:T(1024)S(1)}, f32[1536]{0:T(1024)}, u32[]{:S(2)}) copy-start(f32[1536]{0:T(1024)} %get-tuple-element.28) | copy-start | bytes 18436
  151.9 14.2 %copy-start.23 = (f32[1536]{0:T(1024)S(1)}, f32[1536]{0:T(1024)}, u32[]{:S(2)}) copy-start(f32[1536]{0:T(1024)} %get-tuple-element.29) | copy-start | bytes 18436
  151.9 14.2 %copy-start.24 = (f32[1536]{0:T(1024)S(1)}, f32[1536]{0:T(1024)}, u32[]{:S(2)}) copy-start(f32[1536]{0:T(1024)} %get-tuple-element.30) | copy-start | bytes 18436
  151.9 14.2 %copy-start.25 = (f32[1536]{0:T(1024)S(1)}, f32[1536]{0:T(1024)}, u32[]{:S(2)}) copy-start(f32[1536]{0:T(1024)} %get-tuple-element.31) | copy-start | bytes 18436
  151.9 14.2 %copy-start.26 = (f32[1536]{0:T(1024)S(1)}, f32[1536]{0:T(1024)}, u32[]{:S(2)}) copy-start(f32[1536]{0:T(1024)} %get-tuple-element.32) | copy-start | bytes 18436
  151.9 14.2 %copy-start.28 = (s32[1536]{0:T(1024)S(1)}, s32[1536]{0:T(1024)}, u32[]{:S(2)}) copy-start(s32[1536]{0:T(1024)} %param.24) | copy-start | bytes 18436
  151.9 14.2 %copy-start.30 = (f32[1536]{0:T(1024)S(1)}, f32[1536]{0:T(1024)}, u32[]{:S(2)}) copy-start(f32[1536]{0:T(1024)} %param.23) | copy-start | bytes 18436
  152.0 14.2 %copy-start.37 = (f32[768]{0:T(1024)S(1)}, f32[768]{0:T(1024)}, u32[]{:S(2)}) copy-start(f32[768]{0:T(1024)} %param.18) | copy-start | bytes 9220
  153.6 9.3 %all-to-all-start.5 = ((f32[8,1,768]{2,1,0:T(1,128)}), f32[8,1,768]{2,1,0:T(1,128)S(1)}, u32[]{:S(2)}, u32[]{:S(2)}) async-start(f32[8,1,768]{2,1,0:T(1,128)} %reshape.298), calls=%async_computation.5 | async-start | bytes 49152 | tf_op jit(solution)/shard_map/all_to_all | solution.py:123
  159.0 159.9 %all-reduce.10.cloned.1.call-start = ((), (), s32[]{:S(2)}) async-start(), calls=%async_computation.6 | async-start | bytes 4915200 | tf_op jit(solution)/shard_map/psum | solution.py:138
  165.7 7.5 %slice-start = ((s8[4718592]{0:T(1024)(128)(4,1)}), s8[524288]{0:T(1024)(128)(4,1)S(1)}, s32[]{:S(2)}) async-start(s8[4718592]{0:T(1024)(128)(4,1)} %bitcast.126), calls=%async_computation.7 | async-start | bytes 1048576
  166.2 7.0 %slice-start.1 = ((s8[4718592]{0:T(1024)(128)(4,1)}), s8[4194304]{0:T(1024)(128)(4,1)S(1)}, s32[]{:S(2)}) async-start(s8[4718592]{0:T(1024)(128)(4,1)} %bitcast.126), calls=%async_computation.8 | async-start | bytes 8388608
  173.2 6.2 %copy-start.15 = (bf16[1536,32]{0,1:T(8,128)(2,1)S(1)}, bf16[1536,32]{0,1:T(8,128)(2,1)}, u32[]{:S(2)}) copy-start(bf16[1536,32]{0,1:T(8,128)(2,1)} %param.16) | copy-start | bytes 294916
  179.4 1.2 copy-start.8
  179.4 1.2 copy-start.10
Sparse Core Ops, SparseCore 0:
  180.7 138.1 all-reduce.9
where the time goes:
time: 336 us; the launch traced here: 331 us
  waiting for transfers between devices  86.9 us (26%)
  other arithmetic  69.4 us (21%)
  local copies, waits for them, and re-layouts  60.8 us (18%)
  blocking collectives  44 us (13%)
  starting transfers between devices  32.7 us (10%)
  matrix products  21.9 us (7%)
  between operations  14.9 us (4%)
    psum x1, waiting for transfers between devices, body(): lax.psum(lower_grads(reach_attrs, w_second, saved_acts, g_two), ('basin',...  86.9 us
    psum x1, blocking collectives, body(): lax.psum(lower_grads(reach_attrs, w_second, saved_acts, g_two), ('basin',...  44 us
    scatter-add x3, other arithmetic, body(): confluence_inflow = jnp.zeros((local_events, local_reaches + 1), jnp.floa...  27.6 us
    unnamed x107, local copies, waits for them, and re-layouts  25.7 us
    all_to_all x3, starting transfers between devices, body(): lax.all_to_all(confluence_padded[:, senders], 'basin', split_axis=1, conc...  16.4 us
    all_to_all x3, starting transfers between devices, body(): lax.all_to_all(padded[:, targets], 'basin', split_axis=1, concat_axis=1,...  16.3 us
    gather x6, local copies, waits for them, and re-layouts, body(): g_flow = g_flow[:, :local_reaches] + padded[:, down_local]  15.3 us
    dot_general x1, matrix products, lower_grads(): jnp.dot(g_two, w_second.T, preferred_element_type=jnp.float32)  6.96 us
  transfers between devices with their start and end apart: 7, of which 1 were waited for; matrix products, arithmetic and copies ran while one was open for 18% of the time, Pallas kernels for 0%

commit v1 on v0

v1 whole, which is shorter than its diff:
```python
import functools
import math

import jax
import jax.numpy as jnp
from jax import lax
from jax.experimental import pallas as pl
from jax.experimental.pallas import tpu as pltpu
from jax.sharding import PartitionSpec as P

STEPS = 3
LINKS = 4
GROUP = 32
MESH = pl.DeviceIdType.MESH
NT = (((1,), (1,)), ((), ()))


def split_two(x):
    high = x.astype(jnp.bfloat16)
    low = (x - high.astype(jnp.float32)).astype(jnp.bfloat16)
    return jnp.concatenate([high, low], axis=0)


def kernel(
    n, n_event, owners, chunk, scale,
    w_firstT, w_second, w_secondT, cols, attrs, rows, send_list, recv_list,
    area_start, lateral, cotangent,
    outflow, grad_lateral, full,
    t_one, h_one, d_two, h_two, g_two, squash_row, take_send, take_recv,
    out_msg, in_msg, rate_out, rate_in, slab, rs_in,
    x_send, x_recv, r_send, r_recv, s_send, s_recv, b_send, b_recv, y_send, y_recv, c_send, c_recv,
):
    f32, bf16 = jnp.float32, jnp.bfloat16
    me = lax.axis_index("basin")
    ev = lax.axis_index("event")
    events, reaches = area_start.shape
    hid = w_second.shape[0]
    feat = w_firstT.shape[1]
    part = hid // n_event
    offsets = (1, 2, n // 2, n - 1)
    base = pl.multiple_of(ev * part, 64)

    barrier = pltpu.get_barrier_semaphore()

    @pl.loop(1, n)
    def _(i):
        pl.semaphore_signal(barrier, inc=1, device_id={"basin": lax.rem(me + i, n)}, device_id_type=MESH)

    for i in range(1, n_event):
        pl.semaphore_signal(
            barrier, inc=1, device_id={"event": lax.rem(ev + i, n_event)}, device_id_type=MESH
        )

    tile = 256

    @pl.loop(0, reaches // tile)
    def _(i):
        where = pl.ds(pl.multiple_of(i * tile, tile), tile)
        one = jnp.tanh(
            jnp.dot(w_firstT[...], attrs[0:feat, where], preferred_element_type=f32) + cols[:, 0:1]
        )
        t_one[:, where] = one
        hidden = one.astype(bf16)
        h_one[:, where] = hidden
        two = jnp.tanh(
            jnp.dot(w_secondT[...], hidden, preferred_element_type=f32) + cols[:, 1:2]
        )
        h_two[:, where] = two.astype(bf16)
        d_two[:, where] = cols[:, 2:3] * (1.0 - two * two)
        logit = jnp.sum(two.astype(bf16).astype(f32) * cols[:, 2:3], axis=0, keepdims=True)
        squash_row[:, where] = 1.0 / (1.0 + jnp.exp(-logit))

    slot_row = lax.broadcasted_iota(jnp.int32, (LINKS * GROUP, 1), 0)
    slot = slot_row % GROUP
    cap = send_list.shape[2]
    spread = (
        slot == lax.broadcasted_iota(jnp.int32, (LINKS * GROUP, cap), 1)
    ).astype(f32)
    lane_reach = lax.broadcasted_iota(jnp.int32, (LINKS * GROUP, reaches), 1).astype(f32)
    lane_basin = lax.broadcasted_iota(jnp.int32, (LINKS * GROUP, n), 1)

    def one_hot_of(lists, sign):
        table = lax.dot_general(
            spread, lists[0].astype(f32), NT, precision=lax.Precision.HIGHEST,
            preferred_element_type=f32,
        )
        peer = jnp.zeros((LINKS * GROUP, 1), jnp.int32)
        for k, off in enumerate(offsets):
            peer = jnp.where(slot_row // GROUP == k, lax.rem(me + sign * off + n, n), peer)
        column = jnp.sum(jnp.where(lane_basin == peer, table, 0.0), axis=1, keepdims=True)
        column = jnp.where(slot < cap, column, float(reaches))
        return (jnp.abs(lane_reach - column) < 0.5).astype(bf16)

    take_send[...] = one_hot_of(send_list, 1)
    take_recv[...] = one_hot_of(recv_list, -1)

    squash = squash_row[...]
    rough = 0.02 + 0.08 * squash
    rate = rows[0:1, :] / rough
    beta = rows[1:2, :]
    hop = rows[2:3, :]
    masks = [(jnp.abs(hop - float(d)) < 0.5).astype(f32) for d in range(1, 9)]

    pl.semaphore_wait(barrier, n - 1 + n_event - 1)

    lane_group = lax.broadcasted_iota(jnp.int32, (8, 128), 1) // GROUP
    blocks = events // 8

    def message(index, k, sign):
        return pltpu.make_async_remote_copy(
            src_ref=out_msg.at[index, k],
            dst_ref=in_msg.at[index, k],
            send_sem=x_send.at[index, k],
            recv_sem=x_recv.at[index, k],
            device_id={"basin": lax.rem(me + sign * offsets[k] + n, n)},
            device_id_type=MESH,
        )

    def send(index, field, matrix, sign):
        both = lax.dot_general(split_two(field), matrix[...], NT, preferred_element_type=f32)
        picked = both[:events] + both[events:]
        for k in range(LINKS):
            packed = jnp.zeros((8, 128), f32)
            for q in range(blocks):
                piece = picked[8 * q : 8 * q + 8]
                shift = ((q - k) * GROUP) % 128
                if shift:
                    piece = pltpu.roll(piece, shift, 1)
                packed = jnp.where(lane_group == q, piece, packed)
            out_msg[index, k] = packed
            message(index, k, sign).start()

    def receive(index, matrix, sign):
        for k in range(LINKS):
            message(index, k, sign).wait_recv()
        pieces = []
        for q in range(blocks):
            got = jnp.zeros((8, 128), f32)
            for k in range(LINKS):
                piece = in_msg[index, k]
                shift = ((k - q) * GROUP) % 128
                if shift:
                    piece = pltpu.roll(piece, shift, 1)
                got = jnp.where(lane_group == k, piece, got)
            pieces.append(got)
        both = jnp.dot(
            split_two(jnp.concatenate(pieces, axis=0)), matrix[...], preferred_element_type=f32
        )
        return both[:events] + both[events:]

    def power(area):
        return jnp.exp((2.0 / 3.0) * jnp.log(area))

    areas = [area_start[...]]
    powers = [power(areas[0])]
    shrinks = []
    for t in range(STEPS):
        area, p = areas[t], powers[t]
        flow = rate * area * p
        send(t, flow, take_send, 1)
        inflow = lateral[t]
        for d in range(1, 9):
            inflow = inflow + pltpu.roll(flow * masks[d - 1], d, 1)
        shrink = 1.0 / (1.0 + beta * rate * p)
        shrinks.append(shrink)
        inflow = inflow + receive(t, take_recv, 1)
        areas.append((area + beta * inflow) * shrink)
        powers.append(power(areas[t + 1]))
    emitted = areas[STEPS] * powers[STEPS]
    outflow[...] = rate * emitted
    g_area = cotangent[...] * rate * (5.0 / 3.0) * powers[STEPS]
    g_rate = cotangent[...] * emitted
    for t in reversed(range(STEPS)):
        index = 2 * STEPS - 1 - t
        inner = g_area * shrinks[t]
        g_inflow = inner * beta
        grad_lateral[t] = g_inflow
        send(index, g_inflow, take_recv, -1)
        g_flow = jnp.zeros((events, reaches), f32)
        for d in range(1, 9):
            g_flow = g_flow + masks[d - 1] * pltpu.roll(g_inflow, reaches - d, 1)
        drop = g_inflow * areas[t + 1] * powers[t]
        g_rate = g_rate - drop
        g_area = inner - (2.0 / 3.0) * rate * drop / areas[t]
        g_flow = g_flow + receive(index, take_send, -1)
        g_rate = g_rate + g_flow * areas[t] * powers[t]
        g_area = g_area + (5.0 / 3.0) * rate * powers[t] * g_flow
    rate_out[...] = jnp.sum(g_rate, axis=0, keepdims=True)

    def rate_copy(i):
        return pltpu.make_async_remote_copy(
            src_ref=rate_out,
            dst_ref=rate_in.at[i],
            send_sem=r_send.at[i],
            recv_sem=r_recv.at[i],
            device_id={"event": lax.rem(ev + 1 + i, n_event)},
            device_id_type=MESH,
        )

    for i in range(n_event - 1):
        rate_copy(i).start()
    for i in range(n_event - 1):
        rate_copy(i).wait_recv()
    terms = [rate_out[...]] + [rate_in[i] for i in range(n_event - 1)]
    g_sum = jnp.zeros((1, reaches), f32)
    for e in range(n_event):
        term = terms[0]
        for i in range(n_event - 1):
            term = jnp.where(lax.rem(e + 1 + i, n_event) == ev, terms[i + 1], term)
        g_sum = g_sum + term
    g_logit = (
        g_sum * (-rate / rough) * (scale * 0.08) * squash * (1.0 - squash)
    ).astype(bf16)
    g_logit32 = g_logit.astype(f32)

    @pl.loop(0, hid // 64)
    def _(i):
        where = pl.ds(pl.multiple_of(i * 64, 64), 64)
        g_two[where, :] = (d_two[where, :] * g_logit32).astype(bf16)

    mine = pl.ds(base, part)
    slab[:, 0:hid] = lax.dot_general(h_one[mine, :], g_two[...], NT, preferred_element_type=f32)
    one = t_one[mine, :]
    g_pre = (
        jnp.dot(w_second[mine, :], g_two[...], preferred_element_type=f32) * (1.0 - one * one)
    ).astype(bf16)
    lane_kind = lax.broadcasted_iota(jnp.int32, (128, reaches), 0)
    units = jnp.where(lane_kind == feat + 1, 1.0, 0.0).astype(bf16)
    logits = jnp.where(lane_kind == feat + 2, g_logit32, 0.0).astype(bf16)
    slab[:, hid:] = (
        lax.dot_general(g_pre, attrs[...], NT, preferred_element_type=f32)
        + lax.dot_general(g_two[mine, :], units, NT, preferred_element_type=f32)
        + lax.dot_general(h_two[mine, :], logits, NT, preferred_element_type=f32)
    )

    def when_owner(index, work):
        if owners == n:
            work()
        else:
            pl.when(index < owners)(work)

    def span(index):
        return pl.ds(pl.multiple_of(index * chunk, 8), chunk)

    def scatter_copy(owner, sender):
        return pltpu.make_async_remote_copy(
            src_ref=slab.at[span(owner)],
            dst_ref=rs_in.at[sender],
            send_sem=s_send.at[owner],
            recv_sem=s_recv.at[sender],
            device_id={"basin": owner},
            device_id_type=MESH,
        )

    @pl.loop(1, n)
    def _(i):
        owner = lax.rem(me + i, n)
        when_owner(owner, lambda: scatter_copy(owner, me).start())

    def place(event, index):
        return pl.ds(pl.multiple_of(event * part + index * chunk, 8), chunk)

    def gather_copy(index, peer):
        where = full.at[place(ev, index)]
        return pltpu.make_async_remote_copy(
            src_ref=where, dst_ref=where, send_sem=b_send.at[peer], recv_sem=b_recv.at[index],
            device_id={"basin": peer}, device_id_type=MESH,
        )

    half = lax.rem(ev + n_event // 2, n_event)
    twin = ev + 1 - 2 * lax.rem(ev, 2)
    twin_half = lax.rem(twin + n_event // 2, n_event)

    def half_copy(event, index):
        where = full.at[place(event, index)]
        return pltpu.make_async_remote_copy(
            src_ref=where, dst_ref=where, send_sem=y_send.at[index], recv_sem=y_recv.at[index],
            device_id={"event": half}, device_id_type=MESH,
        )

    def twin_copy(event, index, order):
        where = full.at[place(event, index)]
        return pltpu.make_async_remote_copy(
            src_ref=where, dst_ref=where, send_sem=c_send.at[order, index],
            recv_sem=c_recv.at[order, index],
            device_id={"event": twin}, device_id_type=MESH,
        )

    def own():
        def add(i, total):
            sender = lax.rem(me + n - i, n)
            scatter_copy(me, sender).wait_recv()
            return total + rs_in[sender]

        full[place(ev, me), :] = lax.fori_loop(1, n, add, slab[span(me), :])

        @pl.loop(1, n)
        def _(i):
            gather_copy(me, lax.rem(me + i, n)).start()

        half_copy(ev, me).start()
        twin_copy(ev, me, 0).start()

    when_owner(me, own)

    @pl.loop(1, n)
    def _(i):
        source = lax.rem(me + n - i, n)

        def go():
            gather_copy(source, me).wait_recv()
            half_copy(ev, source).start()
            twin_copy(ev, source, 0).start()

        when_owner(source, go)

    @pl.loop(0, n)
    def _(i):
        source = lax.rem(me + n - i, n)

        def go():
            half_copy(half, source).wait_recv()
            twin_copy(half, source, 1).start()

        when_owner(source, go)

    for index in range(2 * STEPS):
        for k in range(LINKS):
            message(index, k, 1).wait_send()
    for i in range(n_event - 1):
        rate_copy(i).wait_send()

    @pl.loop(1, n)
    def _(i):
        peer = lax.rem(me + i, n)
        when_owner(peer, lambda: scatter_copy(peer, me).wait_send())
        when_owner(me, lambda: gather_copy(me, peer).wait_send())

    @pl.loop(0, owners)
    def _(i):
        half_copy(ev, i).wait_send()
        twin_copy(twin, i, 0).wait_recv()
        twin_copy(twin_half, i, 1).wait_recv()
        twin_copy(ev, i, 0).wait_send()
        twin_copy(half, i, 1).wait_send()


def body(
    n,
    n_event,
    reach_attrs,
    w_first,
    b_first,
    w_second,
    b_second,
    w_out,
    section_factor,
    bed_slope,
    seg_count,
    section_class,
    down_local,
    send_list,
    recv_list,
    area_start,
    lateral,
    cotangent,
):
    f32, bf16 = jnp.float32, jnp.bfloat16
    events, reaches = area_start.shape
    feat, hid = w_first.shape
    class_total = section_factor.shape[0]
    part = hid // n_event
    owners = n if part % (8 * n) == 0 else part // 8
    chunk = part // owners
    scale = 32.0 / math.sqrt(events * n_event * reaches * n)
    one_hot = (section_class[None, :] == jnp.arange(class_total, dtype=jnp.int32)[:, None]).astype(f32)
    k_base = jnp.sqrt(bed_slope) * jnp.sum(one_hot * section_factor[:, None], axis=0)
    position = jnp.arange(reaches, dtype=jnp.int32)
    hop = jnp.where(down_local < reaches, down_local - position, 0).astype(f32)
    rows = jnp.stack([k_base, 1.0 / seg_count.astype(f32), hop], axis=0)
    cols = jnp.stack([b_first, b_second, w_out.astype(f32)], axis=1)
    attrs = jnp.concatenate(
        [reach_attrs.T, jnp.ones((1, reaches), bf16), jnp.zeros((127 - feat, reaches), bf16)], axis=0
    )
    vmem = pl.BlockSpec(memory_space=pltpu.VMEM)
    dma = pltpu.SemaphoreType.DMA
    wide = hid + 128
    outflow, grad_lateral, full = pl.pallas_call(
        functools.partial(kernel, n, n_event, owners, chunk, scale),
        out_shape=(
            jax.ShapeDtypeStruct((events, reaches), f32),
            jax.ShapeDtypeStruct((STEPS, events, reaches), f32),
            jax.ShapeDtypeStruct((hid, wide), f32),
        ),
        in_specs=[vmem] * 11,
        out_specs=(vmem,) * 3,
        scratch_shapes=[
            pltpu.VMEM((hid, reaches), f32),
            pltpu.VMEM((hid, reaches), bf16),
            pltpu.VMEM((hid, reaches), f32),
            pltpu.VMEM((hid, reaches), bf16),
            pltpu.VMEM((hid, reaches), bf16),
            pltpu.VMEM((1, reaches), f32),
            pltpu.VMEM((LINKS * GROUP, reaches), bf16),
            pltpu.VMEM((LINKS * GROUP, reaches), bf16),
            pltpu.VMEM((2 * STEPS, LINKS, 8, 128), f32),
            pltpu.VMEM((2 * STEPS, LINKS, 8, 128), f32),
            pltpu.VMEM((1, reaches), f32),
            pltpu.VMEM((n_event - 1, 1, reaches), f32),
            pltpu.VMEM((part, wide), f32),
            pltpu.VMEM((n, chunk, wide), f32),
            dma((2 * STEPS, LINKS)),
            dma((2 * STEPS, LINKS)),
            dma((n_event - 1,)),
            dma((n_event - 1,)),
            dma((n,)),
            dma((n,)),
            dma((n,)),
            dma((n,)),
            dma((owners,)),
            dma((owners,)),
            dma((2, owners)),
            dma((2, owners)),
        ],
        compiler_params=pltpu.CompilerParams(
            collective_id=0, has_side_effects=True, vmem_limit_bytes=48 * 1024 * 1024
        ),
    )(
        w_first.T, w_second, w_second.T, cols, attrs, rows, send_list, recv_list,
        area_start, lateral, cotangent,
    )
    small = full[:, hid : hid + feat + 3].T
    return (
        outflow,
        grad_lateral,
        small[:feat],
        small[feat],
        full[:, :hid],
        small[feat + 1],
        small[feat + 2],
    )


def solution(mesh):
    return jax.shard_map(
        functools.partial(body, mesh.shape["basin"], mesh.shape["event"]),
        mesh=mesh,
        in_specs=(
            P("basin", None),
            P(),
            P(),
            P(),
            P(),
            P(),
            P(),
            P("basin"),
            P("basin"),
            P("basin"),
            P("basin"),
            P("basin", None, None),
            P("basin", None, None),
            P("event", "basin"),
            P(None, "event", "basin"),
            P("event", "basin"),
        ),
        out_specs=(P("event", "basin"), P(None, "event", "basin"), P(), P(), P(), P(), P()),
        check_vma=False,
    )
```

time: 336 us -> 106 us (0.32); the launches traced: 331 us -> 106 us
  Pallas kernels: 0 us -> 87.8 us
  waiting for transfers between devices: 86.9 us -> 0 us
  other arithmetic: 69.4 us -> 2.37 us
  local copies, waits for them, and re-layouts: 60.8 us -> 14.4 us
  blocking collectives: 44 us -> 0 us
  starting transfers between devices: 32.7 us -> 0 us
  matrix products: 21.9 us -> 0 us
  between operations: 14.9 us -> 0.9 us
    pallas_call x0 -> x1, Pallas kernels: none -> 87.8 us  [body(): pl.pallas_call(functools.partial(kernel, n, n_event, owners, chunk, scale...]
    psum x1 -> x0, waiting for transfers between devices: 86.9 us -> none  [body(): lax.psum(lower_grads(reach_attrs, w_second, saved_acts, g_two), ('basin',...]
    psum x1 -> x0, blocking collectives: 44 us -> none  [body(): lax.psum(lower_grads(reach_attrs, w_second, saved_acts, g_two), ('basin',...]
    scatter-add x9 -> x0, other arithmetic: 40.1 us -> none  [the longest x3 27.6 us: body(): confluence_inflow = jnp.zeros((local_events, local_reaches + 1), jnp.floa...]
    all_to_all x6 -> x0, starting transfers between devices: 32.7 us -> none  [the longest x3 16.4 us: body(): lax.all_to_all(confluence_padded[:, senders], 'basin', split_axis=1, conc...]
    gather x12 -> x0, local copies, waits for them, and re-layouts: 23.8 us -> none  [the longest x6 15.3 us: body(): g_flow = g_flow[:, :local_reaches] + padded[:, down_local]]
    dot_general x7 -> x0, matrix products: 21.9 us -> none  [the longest x1 6.96 us: lower_grads(): jnp.dot(g_two, w_second.T, preferred_element_type=jnp.float32)]
    unnamed x107 -> x35, local copies, waits for them, and re-layouts: 25.7 us -> 8.44 us
  transfers between devices with their start and end apart: 7 -> 0, of which waited for: 1 -> 0; matrix products, arithmetic and copies ran while one was open for 18% -> 0% of each run, Pallas kernels for 0% -> 0%
where the time goes in v1:
time: 106 us
  Pallas kernels  87.8 us (83%)
  local copies, waits for them, and re-layouts  14.4 us (14%)
  other arithmetic  2.37 us (2%)
    pallas_call x1, Pallas kernels, body(): pl.pallas_call(functools.partial(kernel, n, n_event, owners, chunk, scale...  87.8 us
    unnamed x35, local copies, waits for them, and re-layouts  8.44 us
    slice x1, local copies, waits for them, and re-layouts, body(): full[:, :hid]  3.29 us

profile of v1, /device:TPU:21, one launch (start us, length us, event | category | flops | bytes accessed | tf_op | source)
XLA Modules:
  0.0 105.5 jit_solution(9783103891093546108)
XLA Ops:
  0.6 0.0 copy-start
  0.6 0.0 copy-start.14
  0.7 0.0 copy-start.12
  0.7 0.0 copy-start.13
  0.7 0.0 copy-start.10
  0.7 0.0 copy-start.11
  0.7 0.0 copy-start.8
  0.7 0.0 copy-start.9
  0.7 0.0 copy-start.4
  0.7 1.7 %copy.37 = bf16[768,768]{0,1:T(8,128)(2,1)S(1)} copy(bf16[768,768]{1,0:T(8,128)(2,1)} %w_second.1) | data formatting | bytes 2359296 | tf_op args[3]
  2.4 0.0 copy-done.14
  2.4 0.0 copy-done.12
  2.5 0.0 copy-done.13
  2.5 0.2 copy.38.cols
  2.7 0.1 pad.5.clone
  2.8 0.1 pad.4.clone
  2.9 0.0 copy-done.10
  2.9 0.1 maximum_maximum_fusion.attrs
  3.0 1.0 copy.36
  3.9 0.8 select_reduce_fusion
  4.8 0.0 copy-done.11
  4.8 0.7 convert_divide_fusion
  5.5 0.7 select_convert_fusion
  6.3 0.0 copy-done
  6.3 0.0 copy-done.8
  6.3 0.0 copy-done.9
  6.3 0.0 copy-done.4
  6.3 0.0 copy-start.3
  6.3 1.1 %copy-done.3 = f32[3,32,1536]{2,1,0:T(8,128)S(1)} copy-done((f32[3,32,1536]{2,1,0:T(8,128)S(1)}, f32[3,32,1536]{2,1,0:T(8,128)}, u32[]{:S(2)}) %copy-start.3) | copy-done | bytes 589848
  7.4 0.0 copy-start.5
  7.4 0.9 copy-done.5
  8.3 87.8 %shard_map.207 = (f32[32,1536]{1,0:T(8,128)S(1)}, f32[3,32,1536]{2,1,0:T(8,128)S(1)}, f32[768,896]{1,0:T(8,128)}) custom-call(bf16[768,32]{1,0:T(8,128)(2,1)S(1)} %bitcast.8, bf16[768,768]{1,0:T(8,128)(2,1)S(1)} %copy-done, bf16[768,768]{1,0:T(8,128)(2,1)S(1)} %bitcast.7, f32[768,3]{1,0:T(8,128)S(1)} %copy.38.cols, ...), custom_call_target="tpu_custom_call" | custom-call | tf_op jit(solution)/shard_map/pallas_call | solution.py:388
  96.1 0.0 copy-start.1
  96.1 0.8 copy-done.1
  96.9 0.0 copy-start.6
  96.9 0.7 copy-done.6
  97.6 1.0 slice_bitcast_fusion
  98.6 1.3 %slice_reduce_fusion = (f32[768]{0:T(1024)}, f32[768]{0:T(1024)}, f32[768]{0:T(1024)}) fusion(f32[35,768]{0,1:T(8,128)S(1)} %slice_bitcast_fusion), kind=kLoop, calls=%fused_computation | loop fusion | bytes 18432 | tf_op jit(solution)/shard_map/slice | solution.py:440
  99.9 0.8 copy.39
  100.7 0.0 copy-start.7
  100.7 0.0 copy-start.2
  100.7 3.3 %slice.21 = f32[768,768]{1,0:T(8,128)} slice(f32[768,896]{1,0:T(8,128)} %get-tuple-element.12), slice={[0:768], [0:768]} | slice | bytes 4718592 | tf_op jit(solution)/shard_map/slice | solution.py:438
  104.0 0.0 copy-done.7
  104.0 0.7 copy.42
  104.7 0.0 copy-done.2
  104.7 0.8 copy.43
  (10 shorter events, 0.1 us)
Async XLA Ops:
  0.6 5.6 %copy-start = (bf16[768,768]{1,0:T(8,128)(2,1)S(1)}, bf16[768,768]{1,0:T(8,128)(2,1)}, u32[]{:S(2)}) copy-start(bf16[768,768]{1,0:T(8,128)(2,1)} %w_second.1) | copy-start | bytes 3538948
  0.6 1.8 %copy-start.14 = (bf16[768]{0:T(1024)(128)(2,1)S(1)}, bf16[768]{0:T(1024)(128)(2,1)}, u32[]{:S(2)}) copy-start(bf16[768]{0:T(1024)(128)(2,1)} %param.21) | copy-start | bytes 4612
  0.7 1.8 %copy-start.12 = (f32[768]{0:T(1024)S(1)}, f32[768]{0:T(1024)}, u32[]{:S(2)}) copy-start(f32[768]{0:T(1024)} %param.18) | copy-start | bytes 9220
  0.7 1.8 %copy-start.13 = (f32[768]{0:T(1024)S(1)}, f32[768]{0:T(1024)}, u32[]{:S(2)}) copy-start(f32[768]{0:T(1024)} %param.20) | copy-start | bytes 9220
  0.7 2.2 %copy-start.10 = (bf16[1536,32]{0,1:T(8,128)(2,1)S(1)}, bf16[1536,32]{0,1:T(8,128)(2,1)}, u32[]{:S(2)}) copy-start(bf16[1536,32]{0,1:T(8,128)(2,1)} %param.16) | copy-start | bytes 294916
  0.7 4.1 %copy-start.11 = (f32[1536]{0:T(1024)S(1)}, f32[1536]{0:T(1024)}, u32[]{:S(2)}) copy-start(f32[1536]{0:T(1024)} %param.23) | copy-start | bytes 18436
  0.7 5.6 %copy-start.8 = (s32[1,8,24]{2,1,0:T(8,128)S(1)}, s32[1,8,24]{2,1,0:T(8,128)}, u32[]{:S(2)}) copy-start(s32[1,8,24]{2,1,0:T(8,128)} %send_list.1) | copy-start | bytes 2308
  0.7 5.6 %copy-start.9 = (s32[1,8,24]{2,1,0:T(8,128)S(1)}, s32[1,8,24]{2,1,0:T(8,128)}, u32[]{:S(2)}) copy-start(s32[1,8,24]{2,1,0:T(8,128)} %recv_list.1) | copy-start | bytes 2308
  0.7 5.6 %copy-start.4 = (f32[32,1536]{1,0:T(8,128)S(1)}, f32[32,1536]{1,0:T(8,128)}, u32[]{:S(2)}) copy-start(f32[32,1536]{1,0:T(8,128)} %area_start.1) | copy-start | bytes 589828
  6.3 1.1 %copy-start.3 = (f32[3,32,1536]{2,1,0:T(8,128)S(1)}, f32[3,32,1536]{2,1,0:T(8,128)}, u32[]{:S(2)}) copy-start(f32[3,32,1536]{2,1,0:T(8,128)} %lateral.1) | copy-start | bytes 1769476
  7.4 0.9 copy-start.5
  96.1 0.8 copy-start.1
  96.9 0.7 copy-start.6
  100.7 3.3 %copy-start.7 = (f32[32,1536]{1,0:T(8,128)S(1)}, f32[32,1536]{1,0:T(8,128)}, u32[]{:S(2)}) copy-start(f32[32,1536]{1,0:T(8,128)} %copy-done.6) | copy-start | bytes 589828
  100.7 4.0 %copy-start.2 = (f32[3,32,1536]{2,1,0:T(8,128)S(1)}, f32[3,32,1536]{2,1,0:T(8,128)}, u32[]{:S(2)}) copy-start(f32[3,32,1536]{2,1,0:T(8,128)} %copy-done.1) | copy-start | bytes 1769476

commit v2 on v1

--- a/solution.py
+++ b/solution.py
@@ -27,8 +27,10 @@
     area_start, lateral, cotangent,
     outflow, grad_lateral, full,
     t_one, h_one, d_two, h_two, g_two, squash_row, take_send, take_recv,
-    out_msg, in_msg, rate_out, rate_in, slab, rs_in,
-    x_send, x_recv, r_send, r_recv, s_send, s_recv, b_send, b_recv, y_send, y_recv, c_send, c_recv,
+    out_msg, in_msg, rate_out, rate_in, slab, rs_pair, rs_line,
+    x_send, x_recv, r_send, r_recv, px_send, px_recv, pz_send, pz_recv,
+    az_send, az_recv, ax_send, ax_recv, ay_send, ay_recv, ac_send, ac_recv,
+    bz_send, bz_recv, bx_send, bx_recv, by_send, by_recv, bc_send, bc_recv,
 ):
     f32, bf16 = jnp.float32, jnp.bfloat16
     me = lax.axis_index("basin")
@@ -242,87 +244,179 @@
     def span(index):
         return pl.ds(pl.multiple_of(index * chunk, 8), chunk)
 
-    def scatter_copy(owner, sender):
-        return pltpu.make_async_remote_copy(
-            src_ref=slab.at[span(owner)],
-            dst_ref=rs_in.at[sender],
-            send_sem=s_send.at[owner],
-            recv_sem=s_recv.at[sender],
-            device_id={"basin": owner},
-            device_id_type=MESH,
-        )
-
-    @pl.loop(1, n)
-    def _(i):
-        owner = lax.rem(me + i, n)
-        when_owner(owner, lambda: scatter_copy(owner, me).start())
-
-    def place(event, index):
-        return pl.ds(pl.multiple_of(event * part + index * chunk, 8), chunk)
-
-    def gather_copy(index, peer):
-        where = full.at[place(ev, index)]
-        return pltpu.make_async_remote_copy(
-            src_ref=where, dst_ref=where, send_sem=b_send.at[peer], recv_sem=b_recv.at[index],
-            device_id={"basin": peer}, device_id_type=MESH,
-        )
-
+    line = n // 2
+    low = lax.rem(me, 2)
+    spot = me // 2
+    pair = me + 1 - 2 * low
     half = lax.rem(ev + n_event // 2, n_event)
     twin = ev + 1 - 2 * lax.rem(ev, 2)
     twin_half = lax.rem(twin + n_event // 2, n_event)
 
-    def half_copy(event, index):
-        where = full.at[place(event, index)]
+    def device(z, parity):
+        return 2 * z + parity
+
+    def pair_sum(z, parity):
         return pltpu.make_async_remote_copy(
-            src_ref=where, dst_ref=where, send_sem=y_send.at[index], recv_sem=y_recv.at[index],
-            device_id={"event": half}, device_id_type=MESH,
-        )
-
-    def twin_copy(event, index, order):
-        where = full.at[place(event, index)]
+            src_ref=slab.at[span(device(z, parity))], dst_ref=rs_pair.at[z],
+            send_sem=px_send.at[z], recv_sem=px_recv.at[z],
+            device_id={"basin": pair}, device_id_type=MESH,
+        )
+
+    def line_sum(z, sender):
         return pltpu.make_async_remote_copy(
-            src_ref=where, dst_ref=where, send_sem=c_send.at[order, index],
-            recv_sem=c_recv.at[order, index],
-            device_id={"event": twin}, device_id_type=MESH,
-        )
+            src_ref=rs_pair.at[z], dst_ref=rs_line.at[sender],
+            send_sem=pz_send.at[z], recv_sem=pz_recv.at[sender],
+            device_id={"basin": device(z, low)}, device_id_type=MESH,
+        )
+
+    for j in range(line):
+        z = lax.rem(spot + 1 + j, line)
+        when_owner(device(z, 1 - low), lambda z=z: pair_sum(z, 1 - low).start())
+
+    @pl.loop(0, line)
+    def _(j):
+        z = lax.rem(spot + 1 + j, line)
+
+        def go():
+            pair_sum(z, 1 - low).wait_recv()
+            rs_pair[z] = rs_pair[z] + slab[span(device(z, low)), :]
+
+            @pl.when(j < line - 1)
+            def _():
+                line_sum(z, spot).start()
+
+        when_owner(device(z, low), go)
+
+    late = chunk if chunk < 24 else chunk // 24 * 16
+    early = chunk - late
+
+    def rows_a(event, z, parity):
+        return full.at[pl.ds(pl.multiple_of(event * part + device(z, parity) * chunk, 8), late)]
+
+    def rows_b(event, z, parity):
+        start = event * part + device(z, parity) * chunk + late
+        return full.at[pl.ds(pl.multiple_of(start, 8), early)]
+
+    def move(where, send_sem, recv_sem, target):
+        return pltpu.make_async_remote_copy(
+            src_ref=where, dst_ref=where, send_sem=send_sem, recv_sem=recv_sem,
+            device_id=target, device_id_type=MESH,
+        )
+
+    def a_line(source, peer):
+        return move(rows_a(ev, source, low), az_send.at[peer], az_recv.at[source],
+                    {"basin": device(peer, low)})
+
+    def a_pair(z, parity):
+        return move(rows_a(ev, z, parity), ax_send.at[z], ax_recv.at[z], {"basin": pair})
+
+    def a_half(event, z, parity):
+        at = device(z, parity)
+        return move(rows_a(event, z, parity), ay_send.at[at], ay_recv.at[at], {"event": half})
+
+    def a_twin(side, event, z, parity):
+        at = device(z, parity)
+        return move(rows_a(event, z, parity), ac_send.at[side, at], ac_recv.at[side, at],
+                    {"event": twin})
+
+    def b_line(side, source, peer):
+        return move(rows_b((ev, half)[side], source, low), bz_send.at[side, peer],
+                    bz_recv.at[side, source], {"basin": device(peer, low)})
+
+    def b_pair(side, z, parity):
+        return move(rows_b((ev, half)[side], z, parity), bx_send.at[side, z],
+                    bx_recv.at[side, z], {"basin": pair})
+
+    def b_half(event):
+        return move(rows_b(event, spot, low), by_send, by_recv, {"event": half})
+
+    def b_twin(side, event, z, parity):
+        at = device(z, parity)
+        return move(rows_b(event, z, parity), bc_send.at[side, at], bc_recv.at[side, at],
+                    {"event": twin})
+
+    def a_on(z, parity):
+        a_half(ev, z, parity).start()
+        a_twin(0, ev, z, parity).start()
+
+    def b_spread(side):
+        for j in range(1, line):
+            b_line(side, spot, lax.rem(spot + j, line)).start()
+        b_pair(side, spot, low).start()
+        b_twin(side, (ev, half)[side], spot, low).start()
 
     def own():
         def add(i, total):
-            sender = lax.rem(me + n - i, n)
-            scatter_copy(me, sender).wait_recv()
-            return total + rs_in[sender]
-
-        full[place(ev, me), :] = lax.fori_loop(1, n, add, slab[span(me), :])
-
-        @pl.loop(1, n)
-        def _(i):
-            gather_copy(me, lax.rem(me + i, n)).start()
-
-        half_copy(ev, me).start()
-        twin_copy(ev, me, 0).start()
+            sender = lax.rem(spot + line - i, line)
+            line_sum(spot, sender).wait_recv()
+            return total + rs_line[sender]
+
+        full[pl.ds(pl.multiple_of(ev * part + me * chunk, 8), chunk), :] = lax.fori_loop(
+            1, line, add, rs_pair[spot]
+        )
+
+        a_half(ev, spot, low).start()
+        for j in range(1, line):
+            a_line(spot, lax.rem(spot + j, line)).start()
+        a_pair(spot, low).start()
+        a_twin(0, ev, spot, low).start()
+        if early:
+            b_half(ev).start()
+            b_spread(0)
 
     when_owner(me, own)
-
-    @pl.loop(1, n)
-    def _(i):
-        source = lax.rem(me + n - i, n)
+    when_owner(pair, lambda: (a_pair(spot, 1 - low).wait_recv(), a_on(spot, 1 - low))[0])
+    if early:
+        b_half(half).wait_recv()
+        b_spread(1)
+
+    @pl.loop(1, line)
+    def _(j):
+        z = lax.rem(spot + line - j, line)
 
         def go():
-            gather_copy(source, me).wait_recv()
-            half_copy(ev, source).start()
-            twin_copy(ev, source, 0).start()
-
-        when_owner(source, go)
-
-    @pl.loop(0, n)
-    def _(i):
-        source = lax.rem(me + n - i, n)
-
-        def go():
-            half_copy(half, source).wait_recv()
-            twin_copy(half, source, 1).start()
-
-        when_owner(source, go)
+            a_line(z, spot).wait_recv()
+            a_half(ev, z, low).start()
+            a_pair(z, low).start()
+            a_twin(0, ev, z, low).start()
+
+        when_owner(device(z, low), go)
+
+        def go_pair():
+            a_pair(z, 1 - low).wait_recv()
+            a_on(z, 1 - low)
+
+        when_owner(device(z, 1 - low), go_pair)
+
+    if early:
+        for side in range(2):
+            event = (ev, half)[side]
+            b_pair(side, spot, 1 - low).wait_recv()
+            b_twin(side, event, spot, 1 - low).start()
+
+        @pl.loop(1, line)
+        def _(j):
+            z = lax.rem(spot + line - j, line)
+            for side in range(2):
+                event = (ev, half)[side]
+                b_line(side, z, spot).wait_recv()
+                b_pair(side, z, low).start()
+                b_twin(side, event, z, low).start()
+            for side in range(2):
+                event = (ev, half)[side]
+                b_pair(side, z, 1 - low).wait_recv()
+                b_twin(side, event, z, 1 - low).start()
+
+    @pl.loop(0, line)
+    def _(j):
+        z = lax.rem(spot + line - j, line)
+        for parity in (low, 1 - low):
+
+            def go():
+                a_half(half, z, parity).wait_recv()
+                a_twin(1, half, z, parity).start()
+
+            when_owner(device(z, parity), go)
 
     for index in range(2 * STEPS):
         for k in range(LINKS):
@@ -330,19 +424,41 @@
     for i in range(n_event - 1):
         rate_copy(i).wait_send()
 
-    @pl.loop(1, n)
-    def _(i):
-        peer = lax.rem(me + i, n)
-        when_owner(peer, lambda: scatter_copy(peer, me).wait_send())
-        when_owner(me, lambda: gather_copy(me, peer).wait_send())
-
-    @pl.loop(0, owners)
-    def _(i):
-        half_copy(ev, i).wait_send()
-        twin_copy(twin, i, 0).wait_recv()
-        twin_copy(twin_half, i, 1).wait_recv()
-        twin_copy(ev, i, 0).wait_send()
-        twin_copy(half, i, 1).wait_send()
+    @pl.loop(0, line)
+    def _(z):
+        when_owner(device(z, 1 - low), lambda: pair_sum(z, 1 - low).wait_send())
+        when_owner(device(z, low), lambda: a_pair(z, low).wait_send())
+
+        @pl.when(z != spot)
+        def _():
+            when_owner(device(z, low), lambda: line_sum(z, spot).wait_send())
+            when_owner(me, lambda: a_line(spot, z).wait_send())
+
+        if early:
+            for side in range(2):
+                b_pair(side, z, low).wait_send()
+
+                @pl.when(z != spot)
+                def _():
+                    b_line(side, spot, z).wait_send()
+
+        for parity in range(2):
+
+            def go():
+                a_half(ev, z, parity).wait_send()
+                a_twin(0, twin, z, parity).wait_recv()
+                a_twin(1, twin_half, z, parity).wait_recv()
+                a_twin(0, ev, z, parity).wait_send()
+                a_twin(1, half, z, parity).wait_send()
+                if early:
+                    for side in range(2):
+                        b_twin(side, (twin, twin_half)[side], z, parity).wait_recv()
+                        b_twin(side, (ev, half)[side], z, parity).wait_send()
+
+            when_owner(device(z, parity), go)
+
+    if early:
+        b_half(ev).wait_send()
 
 
 def body(
@@ -408,19 +524,32 @@
             pltpu.VMEM((1, reaches), f32),
             pltpu.VMEM((n_event - 1, 1, reaches), f32),
             pltpu.VMEM((part, wide), f32),
-            pltpu.VMEM((n, chunk, wide), f32),
+            pltpu.VMEM((n // 2, chunk, wide), f32),
+            pltpu.VMEM((n // 2, chunk, wide), f32),
             dma((2 * STEPS, LINKS)),
             dma((2 * STEPS, LINKS)),
             dma((n_event - 1,)),
             dma((n_event - 1,)),
+            dma((n // 2,)),
+            dma((n // 2,)),
+            dma((n // 2,)),
+            dma((n // 2,)),
+            dma((n // 2,)),
+            dma((n // 2,)),
+            dma((n // 2,)),
+            dma((n // 2,)),
             dma((n,)),
             dma((n,)),
-            dma((n,)),
-            dma((n,)),
-            dma((owners,)),
-            dma((owners,)),
-            dma((2, owners)),
-            dma((2, owners)),
+            dma((2, n)),
+            dma((2, n)),
+            dma((2, n // 2)),
+            dma((2, n // 2)),
+            dma((2, n // 2)),
+            dma((2, n // 2)),
+            dma,
+            dma,
+            dma((2, n)),
+            dma((2, n)),
         ],
         compiler_params=pltpu.CompilerParams(
             collective_id=0, has_side_effects=True, vmem_limit_bytes=48 * 1024 * 1024

time: 106 us -> 105 us (level)
  the two profiles are of different devices: /device:TPU:21 before, /device:TPU:11 now
where the time goes in v2:
time: 105 us
  Pallas kernels  86.9 us (83%)
  local copies, waits for them, and re-layouts  14.4 us (14%)
  other arithmetic  2.37 us (2%)
    pallas_call x1, Pallas kernels, body(): pl.pallas_call(functools.partial(kernel, n, n_event, owners, chunk, scale...  86.9 us
    unnamed x35, local copies, waits for them, and re-layouts  8.44 us
    slice x1, local copies, waits for them, and re-layouts, body(): full[:, :hid]  3.29 us

profile of v2, /device:TPU:11, one launch (start us, length us, event | category | flops | bytes accessed | tf_op | source)
XLA Modules:
  0.0 104.6 jit_solution(433367075486776292)
XLA Ops:
  0.6 0.0 copy-start
  0.6 0.0 copy-start.14
  0.7 0.0 copy-start.12
  0.7 0.0 copy-start.13
  0.7 0.0 copy-start.10
  0.7 0.0 copy-start.11
  0.7 0.0 copy-start.8
  0.7 0.0 copy-start.9
  0.7 0.0 copy-start.4
  0.7 1.7 %copy.37 = bf16[768,768]{0,1:T(8,128)(2,1)S(1)} copy(bf16[768,768]{1,0:T(8,128)(2,1)} %w_second.1) | data formatting | bytes 2359296 | tf_op args[3]
  2.4 0.0 copy-done.14
  2.4 0.0 copy-done.12
  2.5 0.0 copy-done.13
  2.5 0.2 copy.38.cols
  2.7 0.1 pad.5.clone
  2.8 0.1 pad.4.clone
  2.9 0.0 copy-done.10
  2.9 0.1 maximum_maximum_fusion.attrs
  3.0 1.0 copy.36
  3.9 0.8 select_reduce_fusion
  4.8 0.0 copy-done.11
  4.8 0.7 convert_divide_fusion
  5.5 0.7 select_convert_fusion
  6.3 0.0 copy-done
  6.3 0.0 copy-done.8
  6.3 0.0 copy-done.9
  6.3 0.0 copy-done.4
  6.3 0.0 copy-start.3
  6.3 1.1 %copy-done.3 = f32[3,32,1536]{2,1,0:T(8,128)S(1)} copy-done((f32[3,32,1536]{2,1,0:T(8,128)S(1)}, f32[3,32,1536]{2,1,0:T(8,128)}, u32[]{:S(2)}) %copy-start.3) | copy-done | bytes 589848
  7.4 0.0 copy-start.5
  7.4 0.9 copy-done.5
  8.3 86.9 %shard_map.207 = (f32[32,1536]{1,0:T(8,128)S(1)}, f32[3,32,1536]{2,1,0:T(8,128)S(1)}, f32[768,896]{1,0:T(8,128)}) custom-call(bf16[768,32]{1,0:T(8,128)(2,1)S(1)} %bitcast.8, bf16[768,768]{1,0:T(8,128)(2,1)S(1)} %copy-done, bf16[768,768]{1,0:T(8,128)(2,1)S(1)} %bitcast.7, f32[768,3]{1,0:T(8,128)S(1)} %copy.38.cols, ...), custom_call_target="tpu_custom_call" | custom-call | tf_op jit(solution)/shard_map/pallas_call | solution.py:504
  95.2 0.0 copy-start.1
  95.2 0.8 copy-done.1
  96.0 0.0 copy-start.6
  96.0 0.7 copy-done.6
  96.7 1.0 slice_bitcast_fusion
  97.7 1.3 %slice_reduce_fusion = (f32[768]{0:T(1024)}, f32[768]{0:T(1024)}, f32[768]{0:T(1024)}) fusion(f32[35,768]{0,1:T(8,128)S(1)} %slice_bitcast_fusion), kind=kLoop, calls=%fused_computation | loop fusion | bytes 18432 | tf_op jit(solution)/shard_map/slice | solution.py:569
  99.0 0.8 copy.39
  99.8 0.0 copy-start.7
  99.8 0.0 copy-start.2
  99.8 3.3 %slice.21 = f32[768,768]{1,0:T(8,128)} slice(f32[768,896]{1,0:T(8,128)} %get-tuple-element.12), slice={[0:768], [0:768]} | slice | bytes 4718592 | tf_op jit(solution)/shard_map/slice | solution.py:567
  103.1 0.0 copy-done.7
  103.1 0.7 copy.42
  103.8 0.0 copy-done.2
  103.8 0.8 copy.43
  (10 shorter events, 0.1 us)
Async XLA Ops:
  0.6 5.6 %copy-start = (bf16[768,768]{1,0:T(8,128)(2,1)S(1)}, bf16[768,768]{1,0:T(8,128)(2,1)}, u32[]{:S(2)}) copy-start(bf16[768,768]{1,0:T(8,128)(2,1)} %w_second.1) | copy-start | bytes 3538948
  0.6 1.8 %copy-start.14 = (bf16[768]{0:T(1024)(128)(2,1)S(1)}, bf16[768]{0:T(1024)(128)(2,1)}, u32[]{:S(2)}) copy-start(bf16[768]{0:T(1024)(128)(2,1)} %param.21) | copy-start | bytes 4612
  0.7 1.8 %copy-start.12 = (f32[768]{0:T(1024)S(1)}, f32[768]{0:T(1024)}, u32[]{:S(2)}) copy-start(f32[768]{0:T(1024)} %param.18) | copy-start | bytes 9220
  0.7 1.8 %copy-start.13 = (f32[768]{0:T(1024)S(1)}, f32[768]{0:T(1024)}, u32[]{:S(2)}) copy-start(f32[768]{0:T(1024)} %param.20) | copy-start | bytes 9220
  0.7 2.2 %copy-start.10 = (bf16[1536,32]{0,1:T(8,128)(2,1)S(1)}, bf16[1536,32]{0,1:T(8,128)(2,1)}, u32[]{:S(2)}) copy-start(bf16[1536,32]{0,1:T(8,128)(2,1)} %param.16) | copy-start | bytes 294916
  0.7 4.1 %copy-start.11 = (f32[1536]{0:T(1024)S(1)}, f32[1536]{0:T(1024)}, u32[]{:S(2)}) copy-start(f32[1536]{0:T(1024)} %param.23) | copy-start | bytes 18436
  0.7 5.6 %copy-start.8 = (s32[1,8,24]{2,1,0:T(8,128)S(1)}, s32[1,8,24]{2,1,0:T(8,128)}, u32[]{:S(2)}) copy-start(s32[1,8,24]{2,1,0:T(8,128)} %send_list.1) | copy-start | bytes 2308
  0.7 5.6 %copy-start.9 = (s32[1,8,24]{2,1,0:T(8,128)S(1)}, s32[1,8,24]{2,1,0:T(8,128)}, u32[]{:S(2)}) copy-start(s32[1,8,24]{2,1,0:T(8,128)} %recv_list.1) | copy-start | bytes 2308
  0.7 5.6 %copy-start.4 = (f32[32,1536]{1,0:T(8,128)S(1)}, f32[32,1536]{1,0:T(8,128)}, u32[]{:S(2)}) copy-start(f32[32,1536]{1,0:T(8,128)} %area_start.1) | copy-start | bytes 589828
  6.3 1.1 %copy-start.3 = (f32[3,32,1536]{2,1,0:T(8,128)S(1)}, f32[3,32,1536]{2,1,0:T(8,128)}, u32[]{:S(2)}) copy-start(f32[3,32,1536]{2,1,0:T(8,128)} %lateral.1) | copy-start | bytes 1769476
  7.4 0.9 copy-start.5
  95.2 0.8 copy-start.1
  96.0 0.7 copy-start.6
  99.8 3.3 %copy-start.7 = (f32[32,1536]{1,0:T(8,128)S(1)}, f32[32,1536]{1,0:T(8,128)}, u32[]{:S(2)}) copy-start(f32[32,1536]{1,0:T(8,128)} %copy-done.6) | copy-start | bytes 589828
  99.8 4.0 %copy-start.2 = (f32[3,32,1536]{2,1,0:T(8,128)S(1)}, f32[3,32,1536]{2,1,0:T(8,128)}, u32[]{:S(2)}) copy-start(f32[3,32,1536]{2,1,0:T(8,128)} %copy-done.1) | copy-start | bytes 1769476

commit v3 on v2

--- a/solution.py
+++ b/solution.py
@@ -287,8 +287,8 @@
 
         when_owner(device(z, low), go)
 
-    late = chunk if chunk < 24 else chunk // 24 * 16
-    early = chunk - late
+    early = 0
+    late = chunk - early
 
     def rows_a(event, z, parity):
         return full.at[pl.ds(pl.multiple_of(event * part + device(z, parity) * chunk, 8), late)]

time: 105 us -> 98.7 us (0.940)
  the two profiles are of different devices: /device:TPU:11 before, /device:TPU:21 now
where the time goes in v3:
time: 98.7 us; the launch traced here: 98 us
  Pallas kernels  80.3 us (81%)
  local copies, waits for them, and re-layouts  14.4 us (15%)
  other arithmetic  2.37 us (2%)
    pallas_call x1, Pallas kernels, body(): pl.pallas_call(functools.partial(kernel, n, n_event, owners, chunk, scale...  80.3 us
    unnamed x35, local copies, waits for them, and re-layouts  8.44 us
    slice x1, local copies, waits for them, and re-layouts, body(): full[:, :hid]  3.29 us

profile of v3, /device:TPU:21, one launch (start us, length us, event | category | flops | bytes accessed | tf_op | source)
XLA Modules:
  0.0 98.0 jit_solution(17068427573008819833)
XLA Ops:
  0.6 0.0 copy-start
  0.6 0.0 copy-start.14
  0.7 0.0 copy-start.12
  0.7 0.0 copy-start.13
  0.7 0.0 copy-start.10
  0.7 0.0 copy-start.11
  0.7 0.0 copy-start.8
  0.7 0.0 copy-start.9
  0.7 0.0 copy-start.4
  0.7 1.7 %copy.37 = bf16[768,768]{0,1:T(8,128)(2,1)S(1)} copy(bf16[768,768]{1,0:T(8,128)(2,1)} %w_second.1) | data formatting | bytes 2359296 | tf_op args[3]
  2.4 0.0 copy-done.14
  2.4 0.0 copy-done.12
  2.5 0.0 copy-done.13
  2.5 0.2 copy.38.cols
  2.7 0.1 pad.5.clone
  2.8 0.1 pad.4.clone
  2.9 0.0 copy-done.10
  2.9 0.1 maximum_maximum_fusion.attrs
  3.0 1.0 copy.36
  3.9 0.8 select_reduce_fusion
  4.8 0.0 copy-done.11
  4.8 0.7 convert_divide_fusion
  5.5 0.7 select_convert_fusion
  6.3 0.0 copy-done
  6.3 0.0 copy-done.8
  6.3 0.0 copy-done.9
  6.3 0.0 copy-done.4
  6.3 0.0 copy-start.3
  6.3 1.1 %copy-done.3 = f32[3,32,1536]{2,1,0:T(8,128)S(1)} copy-done((f32[3,32,1536]{2,1,0:T(8,128)S(1)}, f32[3,32,1536]{2,1,0:T(8,128)}, u32[]{:S(2)}) %copy-start.3) | copy-done | bytes 589848
  7.4 0.0 copy-start.5
  7.4 0.9 copy-done.5
  8.3 80.3 %shard_map.207 = (f32[32,1536]{1,0:T(8,128)S(1)}, f32[3,32,1536]{2,1,0:T(8,128)S(1)}, f32[768,896]{1,0:T(8,128)}) custom-call(bf16[768,32]{1,0:T(8,128)(2,1)S(1)} %bitcast.8, bf16[768,768]{1,0:T(8,128)(2,1)S(1)} %copy-done, bf16[768,768]{1,0:T(8,128)(2,1)S(1)} %bitcast.7, f32[768,3]{1,0:T(8,128)S(1)} %copy.38.cols, ...), custom_call_target="tpu_custom_call" | custom-call | tf_op jit(solution)/shard_map/pallas_call | solution.py:504
  88.6 0.0 copy-start.1
  88.6 0.8 copy-done.1
  89.4 0.0 copy-start.6
  89.4 0.7 copy-done.6
  90.1 1.0 %slice_bitcast_fusion = f32[35,768]{0,1:T(8,128)S(1)} fusion(f32[768,896]{1,0:T(8,128)} %get-tuple-element.12), kind=kLoop, calls=%fused_computation.4 | loop fusion | bytes 215040 | tf_op jit(solution)/shard_map/transpose | solution.py:561
  91.1 1.3 %slice_reduce_fusion = (f32[768]{0:T(1024)}, f32[768]{0:T(1024)}, f32[768]{0:T(1024)}) fusion(f32[35,768]{0,1:T(8,128)S(1)} %slice_bitcast_fusion), kind=kLoop, calls=%fused_computation | loop fusion | bytes 18432 | tf_op jit(solution)/shard_map/slice | solution.py:569
  92.4 0.8 copy.39
  93.2 0.0 copy-start.7
  93.2 0.0 copy-start.2
  93.2 3.3 %slice.21 = f32[768,768]{1,0:T(8,128)} slice(f32[768,896]{1,0:T(8,128)} %get-tuple-element.12), slice={[0:768], [0:768]} | slice | bytes 4718592 | tf_op jit(solution)/shard_map/slice | solution.py:567
  96.5 0.0 copy-done.7
  96.5 0.7 copy.42
  97.2 0.0 copy-done.2
  97.2 0.8 copy.43
  (10 shorter events, 0.1 us)
Async XLA Ops:
  0.6 5.6 %copy-start = (bf16[768,768]{1,0:T(8,128)(2,1)S(1)}, bf16[768,768]{1,0:T(8,128)(2,1)}, u32[]{:S(2)}) copy-start(bf16[768,768]{1,0:T(8,128)(2,1)} %w_second.1) | copy-start | bytes 3538948
  0.6 1.8 %copy-start.14 = (bf16[768]{0:T(1024)(128)(2,1)S(1)}, bf16[768]{0:T(1024)(128)(2,1)}, u32[]{:S(2)}) copy-start(bf16[768]{0:T(1024)(128)(2,1)} %param.21) | copy-start | bytes 4612
  0.7 1.8 %copy-start.12 = (f32[768]{0:T(1024)S(1)}, f32[768]{0:T(1024)}, u32[]{:S(2)}) copy-start(f32[768]{0:T(1024)} %param.18) | copy-start | bytes 9220
  0.7 1.8 %copy-start.13 = (f32[768]{0:T(1024)S(1)}, f32[768]{0:T(1024)}, u32[]{:S(2)}) copy-start(f32[768]{0:T(1024)} %param.20) | copy-start | bytes 9220
  0.7 2.2 %copy-start.10 = (bf16[1536,32]{0,1:T(8,128)(2,1)S(1)}, bf16[1536,32]{0,1:T(8,128)(2,1)}, u32[]{:S(2)}) copy-start(bf16[1536,32]{0,1:T(8,128)(2,1)} %param.16) | copy-start | bytes 294916
  0.7 4.1 %copy-start.11 = (f32[1536]{0:T(1024)S(1)}, f32[1536]{0:T(1024)}, u32[]{:S(2)}) copy-start(f32[1536]{0:T(1024)} %param.23) | copy-start | bytes 18436
  0.7 5.6 %copy-start.8 = (s32[1,8,24]{2,1,0:T(8,128)S(1)}, s32[1,8,24]{2,1,0:T(8,128)}, u32[]{:S(2)}) copy-start(s32[1,8,24]{2,1,0:T(8,128)} %send_list.1) | copy-start | bytes 2308
  0.7 5.6 %copy-start.9 = (s32[1,8,24]{2,1,0:T(8,128)S(1)}, s32[1,8,24]{2,1,0:T(8,128)}, u32[]{:S(2)}) copy-start(s32[1,8,24]{2,1,0:T(8,128)} %recv_list.1) | copy-start | bytes 2308
  0.7 5.6 %copy-start.4 = (f32[32,1536]{1,0:T(8,128)S(1)}, f32[32,1536]{1,0:T(8,128)}, u32[]{:S(2)}) copy-start(f32[32,1536]{1,0:T(8,128)} %area_start.1) | copy-start | bytes 589828
  6.3 1.1 %copy-start.3 = (f32[3,32,1536]{2,1,0:T(8,128)S(1)}, f32[3,32,1536]{2,1,0:T(8,128)}, u32[]{:S(2)}) copy-start(f32[3,32,1536]{2,1,0:T(8,128)} %lateral.1) | copy-start | bytes 1769476
  7.4 0.9 copy-start.5
  88.6 0.8 copy-start.1
  89.4 0.7 copy-start.6
  93.2 3.3 %copy-start.7 = (f32[32,1536]{1,0:T(8,128)S(1)}, f32[32,1536]{1,0:T(8,128)}, u32[]{:S(2)}) copy-start(f32[32,1536]{1,0:T(8,128)} %copy-done.6) | copy-start | bytes 589828
  93.2 4.0 %copy-start.2 = (f32[3,32,1536]{2,1,0:T(8,128)S(1)}, f32[3,32,1536]{2,1,0:T(8,128)}, u32[]{:S(2)}) copy-start(f32[3,32,1536]{2,1,0:T(8,128)} %copy-done.1) | copy-start | bytes 1769476
